TPU v7x, 256 devices: a whole 4x4x8 slice. The times are simulated.
256 devices in a mesh: row: 8 (over y, core), col: 8 (over z), dp: 4 (over x).
Axes of the slice: x: 4, y: 4, z: 8, core: 2. Of those that a mesh axis runs over, the one named last changes fastest.
Arguments:
- acts: bfloat16 [2048, 8192], P('dp', 'row'), may hold values from -6 to 6
- cot_hidden: bfloat16 [2048, 15360], P(('dp', 'row'), 'col'), may hold values from -6 to 6
- gate_pre: bfloat16 [2048, 15360], P(('dp', 'row'), 'col'), may hold values from -6 to 6
- up_pre: bfloat16 [2048, 15360], P(('dp', 'row'), 'col'), may hold values from -6 to 6
- w_gate: bfloat16 [8192, 15360], P('row', 'col'), may hold values from -0.0625 to 0.0625
- w_up: bfloat16 [8192, 15360], P('row', 'col'), may hold values from -0.0625 to 0.0625
- gate_down_factor: bfloat16 [8192, 64], replicated, may hold values from -0.0625 to 0.0625
- up_down_factor: bfloat16 [8192, 64], replicated, may hold values from -0.0625 to 0.0625
- b_gate: bfloat16 [64, 15360], P(None, 'col'), may hold values from -0.09375 to 0.09375
- b_up: bfloat16 [64, 15360], P(None, 'col'), may hold values from -0.09375 to 0.09375
Outputs:
- normed_input_gradient: bfloat16 [2048, 8192], P(('dp', 'col'), 'row')
- grad_a_gate: float32 [8192, 64], P(('row', 'col', 'dp'))
- grad_a_up: float32 [8192, 64], P(('row', 'col', 'dp'))
- grad_b_gate: float32 [64, 15360], P(None, ('col', 'row', 'dp'))
- grad_b_up: float32 [64, 15360], P(None, ('col', 'row', 'dp'))
All inputs are finite; a program needn't handle non-finite values.
Results may differ from a plain program's by a relative error of at most 0.012.
Values may be sent and summed in bfloat16 or wider, within the bound.
A program may use at most 64 MiB of HBM per device.

v0:
```python
import jax
import jax.numpy as jnp
from jax import lax
from jax.sharding import PartitionSpec as P

ADAPTER_SCALE = 2.0


def gated_back(cot_hidden, gate_pre, up_pre):
    gate_f = gate_pre.astype(jnp.float32)
    sig = jax.nn.sigmoid(gate_f)
    hid = cot_hidden.astype(jnp.float32)
    d_gate = (hid * up_pre.astype(jnp.float32) * sig * (1.0 + gate_f * (1.0 - sig))).astype(
        jnp.bfloat16
    )
    d_up = (hid * gate_f * sig).astype(jnp.bfloat16)
    return (d_gate, d_up)


def multiply_transposed(left, right):
    return lax.dot_general(
        left, right, (((1,), (1,)), ((), ())), preferred_element_type=jnp.float32
    )


def trans_times(left, right):
    return lax.dot_general(
        left, right, (((0,), (0,)), ((), ())), preferred_element_type=jnp.float32
    )


def on_device(
    acts, cot_hidden, gate_pre, up_pre, w_gate, w_up, gate_down_factor, up_down_factor, b_gate, b_up
):
    group_tok = acts.shape[0]
    width_rows = acts.shape[1]
    own_tok = gate_pre.shape[0]
    row_at = lax.axis_index("row")
    col_at = lax.axis_index("col")
    own_gate, own_up = gated_back(cot_hidden, gate_pre, up_pre)
    full_gate, full_up = (
        lax.all_gather(own_gate, "row", axis=0, tiled=True),
        lax.all_gather(own_up, "row", axis=0, tiled=True),
    )
    gate_factor_rows = lax.dynamic_slice_in_dim(
        gate_down_factor, row_at * width_rows, width_rows, 0
    )
    up_factor_rows = lax.dynamic_slice_in_dim(up_down_factor, row_at * width_rows, width_rows, 0)
    factor = 2.0 / (group_tok * lax.axis_size("dp"))
    out_rows = group_tok // lax.axis_size("col")
    gate_rank_projection, up_rank_projection = lax.psum(
        (multiply_transposed(full_gate, b_gate), multiply_transposed(full_up, b_up)), "col"
    )
    gate_rank_projection = gate_rank_projection.astype(jnp.bfloat16)
    up_rank_projection = up_rank_projection.astype(jnp.bfloat16)
    low_gate, low_up = lax.psum(
        (
            jnp.dot(acts, gate_factor_rows, preferred_element_type=jnp.float32),
            jnp.dot(acts, up_factor_rows, preferred_element_type=jnp.float32),
        ),
        "row",
    )
    low_gate = low_gate.astype(jnp.bfloat16)
    low_up = low_up.astype(jnp.bfloat16)
    frozen_term = lax.psum_scatter(
        multiply_transposed(full_gate, w_gate) + multiply_transposed(full_up, w_up),
        "col",
        scatter_dimension=0,
        tiled=True,
    )
    local_gate_part = lax.dynamic_slice_in_dim(gate_rank_projection, col_at * out_rows, out_rows, 0)
    local_up_part = lax.dynamic_slice_in_dim(up_rank_projection, col_at * out_rows, out_rows, 0)
    adapter_term = multiply_transposed(local_gate_part, gate_factor_rows) + multiply_transposed(
        local_up_part, up_factor_rows
    )
    normed_input_gradient = (frozen_term + ADAPTER_SCALE * adapter_term).astype(jnp.bfloat16)
    sub_width = width_rows // lax.axis_size("col")
    acts_sub = lax.dynamic_slice_in_dim(acts, col_at * sub_width, sub_width, 1)
    grad_a_gate, grad_a_up = (
        lax.psum_scatter(
            factor * trans_times(acts_sub, gate_rank_projection),
            "dp",
            scatter_dimension=0,
            tiled=True,
        ),
        lax.psum_scatter(
            factor * trans_times(acts_sub, up_rank_projection),
            "dp",
            scatter_dimension=0,
            tiled=True,
        ),
    )
    low_own_gate = lax.dynamic_slice_in_dim(low_gate, row_at * own_tok, own_tok, 0)
    low_own_up = lax.dynamic_slice_in_dim(low_up, row_at * own_tok, own_tok, 0)
    column_terms = (
        factor * trans_times(low_own_gate, own_gate),
        factor * trans_times(low_own_up, own_up),
    )
    grad_b_gate, grad_b_up = (
        lax.psum_scatter(column_terms[0], ("row", "dp"), scatter_dimension=1, tiled=True),
        lax.psum_scatter(column_terms[1], ("row", "dp"), scatter_dimension=1, tiled=True),
    )
    return (normed_input_gradient, grad_a_gate, grad_a_up, grad_b_gate, grad_b_up)


def solution(mesh):
    in_specs = (
        P("dp", "row"),
        P(("dp", "row"), "col"),
        P(("dp", "row"), "col"),
        P(("dp", "row"), "col"),
        P("row", "col"),
        P("row", "col"),
        P(),
        P(),
        P(None, "col"),
        P(None, "col"),
    )
    out_specs = (
        P(("dp", "col"), "row"),
        P(("row", "col", "dp"), None),
        P(("row", "col", "dp"), None),
        P(None, ("col", "row", "dp")),
        P(None, ("col", "row", "dp")),
    )
    return jax.shard_map(
        on_device, mesh=mesh, in_specs=in_specs, out_specs=out_specs, check_vma=False
    )
```

profile of v0, /device:TPU:6, one launch (start us, length us, event | category | flops | bytes accessed | tf_op | source)
XLA Modules:
  0.0 254.3 jit_solution(7711121083239397411)
XLA Ops:
  8.0 0.0 all-gather.3.cloned.1.call-start
  8.1 2.4 fusion.11
  10.5 0.0 all-gather.5.cloned.1.call-start
  10.6 0.7 all-gather.5.cloned.1.call-update
  11.3 0.0 all-reduce.9.cloned.1.call-start
  11.3 1.8 convolution_bitcast_fusion
  13.1 0.4 convolution_bitcast_fusion.1
  13.5 30.0 %all-reduce.10 = (bf16[512,64]{0,1:T(8,128)(2,1)S(1)}, bf16[512,64]{0,1:T(8,128)(2,1)S(1)}) all-reduce(f32[512,64]{0,1:T(8,128)S(1)} %convolution_bitcast_fusion.1, f32[512,64]{0,1:T(8,128)S(1)} %convolution_bitcast_fusion), channel_id=1, replica_groups=mesh['row'=8,'col'=8,'dp'=4] {'row'}, use_global_device_ids=true, to_apply=%region_5.0 | all-reduce | flops 65536 | bytes 393216 | tf_op jit(solution)/shard_map/psum | solution.py:56
  43.5 1.1 convolution_multiply_fusion
  44.6 1.1 convolution_multiply_fusion.1
  45.7 0.0 reduce-scatter.6.cloned.1.call-start
  45.7 0.0 all-gather.3.cloned.1.call-done
  45.8 6.4 %fusion.29 = f32[512,1024]{1,0:T(8,128)} fusion(bf16[512,1920]{1,0:T(8,128)(2,1)} %all-gather.3.cloned.1.call-done, bf16[1024,1920]{1,0:T(8,128)(2,1)} %param.14), kind=kOutput, calls=%fused_computation.45 | convolution fusion | flops 2013265920 | bytes 7995392 | tf_op jit(solution)/shard_map/dot_general | solution.py:21
  52.2 19.8 %all-gather.5.cloned.1.call-done = bf16[512,1920]{1,0:T(8,128)(2,1)} async-done(((bf16[64,1920]{1,0:T(8,128)(2,1)}), bf16[512,1920]{1,0:T(8,128)(2,1)}) %all-gather.5.cloned.1.call-update) | async-done | bytes 1966096 | tf_op jit(solution)/shard_map/all_gather | solution.py:43
  72.0 7.1 %convolution_add_fusion = f32[512,1024]{1,0:T(8,128)} fusion(f32[512,1024]{1,0:T(8,128)} %fusion.29, bf16[512,1920]{1,0:T(8,128)(2,1)} %all-gather.5.cloned.1.call-done, bf16[1024,1920]{1,0:T(8,128)(2,1)} %param.15), kind=kOutput, calls=%fused_computation.2 | convolution fusion | flops 2013790208 | bytes 10092544 | tf_op jit(solution)/shard_map/dot_general | solution.py:21
  79.2 0.0 reduce-scatter.10.cloned.1.call-start
  79.2 0.6 copy-done.7
  79.8 0.6 dynamic-slice
  81.0 83.4 %all-reduce.9.cloned.1.call-done = (f32[64,1920]{1,0:T(8,128)}, f32[64,1920]{1,0:T(8,128)}) async-done(((f32[64,1920]{1,0:T(8,128)}, f32[64,1920]{1,0:T(8,128)}), (f32[64,1920]{1,0:T(8,128)}, f32[64,1920]{1,0:T(8,128)})) %all-reduce.9.cloned.1.call-update) | async-done | bytes 983056
  164.4 1.7 constant_dynamic-slice_fusion
  166.1 2.3 fusion.30
  168.4 0.7 fusion.31
  169.1 33.6 %all-reduce.11 = (bf16[512,64]{0,1:T(8,128)(2,1)S(1)}, bf16[512,64]{0,1:T(8,128)(2,1)S(1)}) all-reduce(f32[512,64]{0,1:T(8,128)S(1)} %fusion.30, f32[512,64]{0,1:T(8,128)S(1)} %fusion.31), channel_id=1, replica_groups=mesh['row'=8,'col'=8,'dp'=4] {'col'}, use_global_device_ids=true, to_apply=%region_1.0 | all-reduce | flops 65536 | bytes 393216 | tf_op jit(solution)/shard_map/psum | solution.py:51
  202.7 0.9 convolution_multiply_fusion.2
  203.6 0.9 convolution_multiply_fusion.3
  204.4 0.0 reduce-scatter.8.cloned.1.call-start
  204.5 0.3 fusion.17
  204.8 0.2 reduce-scatter.8.cloned.1.call-update
  205.0 0.0 reduce-scatter.6.cloned.1.call-done
  205.1 2.0 fusion.2
  207.0 14.4 %reduce-scatter.10.cloned.1.call-done = f32[32,64]{1,0:T(8,128)} async-done(((f32[128,64]{1,0:T(8,128)}), f32[32,64]{1,0:T(8,128)}) %reduce-scatter.10.cloned.1.call-update) | async-done | bytes 8208 | tf_op jit(solution)/shard_map/reduce_scatter | solution.py:86
  221.5 25.7 %reduce-scatter.8.cloned.1.call-done = f32[32,64]{1,0:T(8,128)} async-done(((f32[128,64]{1,0:T(8,128)}), f32[32,64]{1,0:T(8,128)}) %reduce-scatter.8.cloned.1.call-update) | async-done | bytes 8208 | tf_op jit(solution)/shard_map/reduce_scatter | solution.py:80
  (19 shorter events, 0.1 us)
Async XLA Ops:
  8.0 5.1 %copy-start = (bf16[8192,64]{0,1:T(8,128)(2,1)S(1)}, bf16[8192,64]{0,1:T(8,128)(2,1)}, u32[]{:S(2)}) copy-start(bf16[8192,64]{0,1:T(8,128)(2,1)} %param.16) | copy-start | bytes 3145732
  8.0 5.1 %copy-start.1 = (bf16[512,1024]{1,0:T(8,128)(2,1)S(1)}, bf16[512,1024]{1,0:T(8,128)(2,1)}, u32[]{:S(2)}) copy-start(bf16[512,1024]{1,0:T(8,128)(2,1)} %param.10) | copy-start | bytes 3145732
  8.0 37.7 %all-gather.3.cloned.1.call-start = ((), (), s32[]{:S(2)}) async-start(), calls=%async_computation.3 | async-start | bytes 2211840 | tf_op jit(solution)/shard_map/all_gather | solution.py:42
  10.5 33.0 %copy-start.2 = (bf16[64,1920]{1,0:T(8,128)(2,1)S(1)}, bf16[64,1920]{1,0:T(8,128)(2,1)}, u32[]{:S(2)}) copy-start(bf16[64,1920]{1,0:T(8,128)(2,1)} %get-tuple-element.11) | copy-start | bytes 737284
  10.5 34.1 %copy-start.3 = (bf16[64,1920]{1,0:T(8,128)(2,1)S(1)}, bf16[64,1920]{1,0:T(8,128)(2,1)}, u32[]{:S(2)}) copy-start(bf16[64,1920]{1,0:T(8,128)(2,1)} %get-tuple-element.12) | copy-start | bytes 737284
  10.5 61.5 %all-gather.5.cloned.1.call-start = ((), (), s32[]{:S(2)}) async-start(), calls=%async_computation.4 | async-start | bytes 2211840 | tf_op jit(solution)/shard_map/all_gather | solution.py:43
  11.3 153.1 %all-reduce.9.cloned.1.call-start = ((), (), s32[]{:S(2)}) async-start(), calls=%async_computation.8 | async-start | bytes 1966080
  45.7 159.4 %reduce-scatter.6.cloned.1.call-start = ((), (), s32[]{:S(2)}) async-start(), calls=%async_computation.5 | async-start | bytes 2359296 | tf_op jit(solution)/shard_map/reduce_scatter | solution.py:65
  79.1 0.7 copy-start.7
  79.1 87.0 %copy-start.5 = (bf16[64,1920]{1,0:T(8,128)(2,1)S(1)}, bf16[64,1920]{1,0:T(8,128)(2,1)}, u32[]{:S(2)}) copy-start(bf16[64,1920]{1,0:T(8,128)(2,1)} %param.18) | copy-start | bytes 737284
  79.1 89.3 %copy-start.6 = (bf16[64,1920]{1,0:T(8,128)(2,1)S(1)}, bf16[64,1920]{1,0:T(8,128)(2,1)}, u32[]{:S(2)}) copy-start(bf16[64,1920]{1,0:T(8,128)(2,1)} %param.19) | copy-start | bytes 737284
  79.2 142.3 %reduce-scatter.10.cloned.1.call-start = ((), (), s32[]{:S(2)}) async-start(), calls=%async_computation.7 | async-start | bytes 81920 | tf_op jit(solution)/shard_map/reduce_scatter | solution.py:86
  164.4 4.0 %copy-start.4 = (bf16[512,1920]{1,0:T(8,128)(2,1)S(1)}, bf16[512,1920]{1,0:T(8,128)(2,1)}, u32[]{:S(2)}) copy-start(bf16[512,1920]{1,0:T(8,128)(2,1)} %all-gather.5.cloned.1.call-done) | copy-start | bytes 5898244
  204.4 42.8 %reduce-scatter.8.cloned.1.call-start = ((), (), s32[]{:S(2)}) async-start(), calls=%async_computation.6 | async-start | bytes 81920 | tf_op jit(solution)/shard_map/reduce_scatter | solution.py:80
Sparse Core Ops, SparseCore 0:
  10.7 31.0 all-gather.2
  43.6 28.3 all-gather.4
  79.3 42.2 reduce-scatter.5
  204.6 16.8 reduce-scatter.9
  224.6 22.5 reduce-scatter.7
Sparse Core Ops, SparseCore 1:
  45.8 118.6 all-reduce.8
where the time goes:
time: 256 us; the launch traced here: 254 us
  waiting for transfers between devices  144 us (56%)
  blocking collectives  63.6 us (25%)
  matrix products  24.8 us (10%)
  between operations  16 us (6%)
  local copies, waits for them, and re-layouts  2.94 us (1%)
    unnamed x7, waiting for transfers between devices  84.4 us
    psum x1, blocking collectives, on_device(): lax.psum((multiply_transposed(full_gate, b_gate), multiply_transposed(ful...  33.6 us
    psum x1, blocking collectives, on_device(): lax.psum((jnp.dot(acts, gate_factor_rows, preferred_element_type=jnp.floa...  30 us
    reduce_scatter x1, waiting for transfers between devices, on_device(): lax.psum_scatter(factor * trans_times(acts_sub, gate_rank_projection), 'd...  25.7 us
    all_gather x1, waiting for transfers between devices, on_device(): lax.all_gather(own_up, 'row', axis=0, tiled=True)  19.8 us
    dot_general x6, matrix products, multiply_transposed(): lax.dot_general(left, right, (((1,), (1,)), ((), ())), preferred_element_...  18.7 us
    reduce_scatter x1, waiting for transfers between devices, on_device(): lax.psum_scatter(factor * trans_times(acts_sub, up_rank_projection), 'dp'...  14.4 us
  transfers between devices with their start and end apart: 6, of which 4 were waited for; matrix products, arithmetic and copies ran while one was open for 11% of the time, Pallas kernels for 0%

commit v1 on v0

v1 whole, which is shorter than its diff:
```python
import jax
import jax.numpy as jnp
from jax import lax
from jax.experimental import pallas as pl
from jax.experimental.pallas import tpu as pltpu
from jax.sharding import PartitionSpec as P

MESH = pl.DeviceIdType.MESH
F32, BF16 = jnp.float32, jnp.bfloat16
ADAPTER_SCALE = 2.0
NY, NZ, NX = 4, 8, 4
ROWS = 2 * NY
CHUNK = 16


def times_transposed(left, right):
    return lax.dot_general(
        left, right, (((1,), (1,)), ((), ())), preferred_element_type=F32
    )


def kernel(
    acts,
    cot,
    gate_pre,
    up_pre,
    w_gate,
    w_up,
    gate_factor,
    up_factor,
    b_gate,
    b_up,
    out,
    ga_gate,
    ga_up,
    gb_gate,
    gb_up,
    pre,
    w,
    b,
    fac,
    act_rows,
    act_cols,
    d,
    part,
    first,
    zm,
    zp,
    adapter,
    rank_part,
    rank_all,
    low_part,
    low_piece,
    low_sum,
    low_all,
    ga_send,
    ga_recv,
    gb_send,
    gb_recv,
    in_sem,
    y_send,
    y_recv,
    p_send,
    p_recv,
    z_send,
    z_recv,
    rz_send,
    rz_recv,
    ry_send,
    ry_recv,
    rp_send,
    rp_recv,
    ls_send,
    ls_recv,
    lg_send,
    lg_recv,
    lz_send,
    lz_recv,
    ga_ssem,
    ga_rsem,
    gb_ssem,
    gb_rsem,
):
    own_tok, hid = cot.shape
    group_tok, width = acts.shape
    n_chunk = own_tok // CHUNK
    factor = 2.0 / (group_tok * NX)
    r, c, x = lax.axis_index("row"), lax.axis_index("col"), lax.axis_index("dp")
    y, core = r // 2, r % 2

    def row_of(step):
        return ((y + step) % NY) * 2 + core

    right, left, far = row_of(1), row_of(NY - 1), row_of(2)
    partner = y * 2 + (1 - core)

    width_at = pl.multiple_of(r * width, width)
    sub = width // NZ
    loads = [
        pltpu.make_async_copy(cot, pre.at[0], in_sem.at[0]),
        pltpu.make_async_copy(gate_pre, pre.at[1], in_sem.at[1]),
        pltpu.make_async_copy(up_pre, pre.at[2], in_sem.at[2]),
        pltpu.make_async_copy(b_gate, b.at[0:64, 0:hid], in_sem.at[3]),
        pltpu.make_async_copy(b_up, b.at[64:128, hid : 2 * hid], in_sem.at[4]),
        pltpu.make_async_copy(
            acts.at[pl.ds(pl.multiple_of(c * own_tok, own_tok), own_tok), :], act_rows, in_sem.at[5]
        ),
        pltpu.make_async_copy(
            gate_factor.at[:, pl.ds(width_at, width)], fac.at[0:64], in_sem.at[6]
        ),
        pltpu.make_async_copy(
            up_factor.at[:, pl.ds(width_at, width)], fac.at[64:128], in_sem.at[7]
        ),
        pltpu.make_async_copy(
            acts.at[:, pl.ds(pl.multiple_of(c * sub, sub), sub)], act_cols, in_sem.at[8]
        ),
        pltpu.make_async_copy(w_gate, w.at[:, 0:hid], in_sem.at[9]),
        pltpu.make_async_copy(w_up, w.at[:, hid : 2 * hid], in_sem.at[10]),
    ]
    for load in loads:
        load.start()

    barrier = pltpu.get_barrier_semaphore()
    for step in range(1, ROWS):
        pl.semaphore_signal(barrier, 1, device_id={"row": (r + step) % ROWS}, device_id_type=MESH)
    for step in range(1, NZ):
        pl.semaphore_signal(barrier, 1, device_id={"col": (c + step) % NZ}, device_id_type=MESH)
    for step in range(1, NX):
        pl.semaphore_signal(barrier, 1, device_id={"dp": (x + step) % NX}, device_id_type=MESH)

    sent = []

    def remote(src, dst, ssem, rsem, **where):
        return pltpu.make_async_remote_copy(
            src_ref=src,
            dst_ref=dst,
            send_sem=ssem,
            recv_sem=rsem,
            device_id=where,
            device_id_type=MESH,
        )

    def start(copy):
        copy.start()
        sent.append(copy)

    def cotangents(q):
        rows = slice(q * CHUNK, (q + 1) * CHUNK)
        gate = pre[1, rows, :].astype(F32)
        sig = jax.nn.sigmoid(gate)
        hot = pre[0, rows, :].astype(F32)
        up = pre[2, rows, :].astype(F32)
        d[q, r, :, 0:hid] = (hot * up * sig * (1.0 + gate * (1.0 - sig))).astype(BF16)
        d[q, r, :, hid : 2 * hid] = (hot * gate * sig).astype(BF16)

    def y_copy(q, kind):
        if kind == 0:
            ref, to = d.at[q, r], right
        elif kind == 1:
            ref, to = d.at[q, r], left
        elif kind == 2:
            ref, to = d.at[q, left, :, 0:hid], right
        else:
            ref, to = d.at[q, right, :, hid : 2 * hid], left
        return remote(ref, ref, y_send.at[q, kind], y_recv.at[q, kind], row=to)

    def p_copy(q, kind):
        ref = d.at[q, (r, left, right, far)[kind]]
        return remote(ref, ref, p_send.at[q, kind], p_recv.at[q, kind], row=partner)

    def own(q):
        start(y_copy(q, 0))
        start(y_copy(q, 1))

    def near(q):
        y_copy(q, 0).wait_recv()
        start(y_copy(q, 2))
        y_copy(q, 1).wait_recv()
        start(y_copy(q, 3))

    def near_partner(q):
        start(p_copy(q, 1))
        start(p_copy(q, 2))

    def far_in(q):
        y_copy(q, 2).wait_recv()
        y_copy(q, 3).wait_recv()
        start(p_copy(q, 3))

    def product(q):
        for kind in range(4):
            p_copy(q, kind).wait_recv()

        @pl.loop(0, width // 256)
        def _(n):
            at = pl.ds(pl.multiple_of(n * 256, 256), 256)
            tile = times_transposed(d[q].reshape(ROWS * CHUNK, 2 * hid), w[at, :])
            part[q, :, :, at] = tile.reshape(ROWS, CHUNK, 256)

    half = width // 2

    def z_copy(q, step, minus):
        if step == 0:
            cols = slice(0, half) if minus else slice(half, width)
            src = first.at[q, :, cols]
            dst = (zm if minus else zp).at[q, 0, :, cols]
        else:
            src = (zm if minus else zp).at[q, step - 1]
            dst = (zm if minus else zp).at[q, step]
        side = 0 if minus else 1
        to = (c + NZ - 1) % NZ if minus else (c + 1) % NZ
        return remote(src, dst, z_send.at[q, step, side], z_recv.at[q, step, side], col=to)

    def z_step(q, step):
        if step == 0:
            first[q] = part[q, (c + 4) % NZ].astype(BF16)
        else:
            z_copy(q, step - 1, True).wait_recv()
            before, after = (c + NZ - (4 - step)) % NZ, (c + (4 - step)) % NZ
            if step == 1:
                lo, hi = slice(0, half), slice(half, width)
                zm[q, 0, :, lo] = (zm[q, 0, :, lo].astype(F32) + part[q, before, :, lo]).astype(BF16)
                zm[q, 0, :, hi] = part[q, before, :, hi].astype(BF16)
            else:
                zm[q, step - 1] = (zm[q, step - 1].astype(F32) + part[q, before]).astype(BF16)
        start(z_copy(q, step, True))
        if step > 0:
            z_copy(q, step - 1, False).wait_recv()
            if step == 1:
                zp[q, 0, :, hi] = (zp[q, 0, :, hi].astype(F32) + part[q, after, :, hi]).astype(BF16)
                zp[q, 0, :, lo] = part[q, after, :, lo].astype(BF16)
            else:
                zp[q, step - 1] = (zp[q, step - 1].astype(F32) + part[q, after]).astype(BF16)
        start(z_copy(q, step, False))

    def z_last(q):
        z_copy(q, 3, True).wait_recv()
        z_copy(q, 3, False).wait_recv()
        rows = slice(q * CHUNK, (q + 1) * CHUNK)
        total = part[q, c] + zm[q, 3].astype(F32) + zp[q, 3].astype(F32) + adapter[rows, :]
        out[rows, :] = total.astype(BF16)

    def rank_z(step):
        ref = rank_part.at[c]
        return remote(
            ref, ref, rz_send.at[step - 1], rz_recv.at[step - 1], col=(c + step) % NZ
        )

    def rank_y(step):
        ref = rank_all.at[y, core]
        return remote(ref, ref, ry_send.at[step - 1], ry_recv.at[step - 1], row=row_of(step))

    def rank_p():
        ref = rank_all.at[:, core]
        return remote(ref, ref, rp_send, rp_recv, row=partner)

    def low_s(step):
        to = (r + step) % ROWS
        return remote(
            low_part.at[pl.ds(pl.multiple_of(to * 8, 8), 8), :],
            low_piece.at[step],
            ls_send.at[step - 1],
            ls_recv.at[step - 1],
            row=to,
        )

    def low_g(step):
        ref = low_sum.at[r]
        return remote(ref, ref, lg_send.at[step - 1], lg_recv.at[step - 1], row=(r + step) % ROWS)

    def low_z(step):
        ref = low_all.at[c]
        return remote(ref, ref, lz_send.at[step - 1], lz_recv.at[step - 1], col=(c + step) % NZ)

    def ga_copy(step):
        to = (x + step) % NX
        return remote(
            ga_send.at[to], ga_recv.at[step], ga_ssem.at[step - 1], ga_rsem.at[step - 1], dp=to
        )

    def gb_copy(step):
        to = (x + step) % NX
        return remote(
            gb_send.at[to], gb_recv.at[step], gb_ssem.at[step - 1], gb_rsem.at[step - 1], dp=to
        )

    for load in loads[0:3]:
        load.wait()
    cotangents(0)
    pl.semaphore_wait(barrier, (ROWS - 1) + (NZ - 1) + (NX - 1))
    own(0)
    cotangents(1)
    own(1)
    cotangents(2)
    cotangents(3)
    for q in range(n_chunk):
        start(p_copy(q, 0))

    b[0:64, hid : 2 * hid] = jnp.zeros((64, hid), BF16)
    b[64:128, 0:hid] = jnp.zeros((64, hid), BF16)
    for load in loads[3:8]:
        load.wait()
    rank_part[c] = times_transposed(d[:, r].reshape(own_tok, 2 * hid), b[...]).astype(BF16)
    for step in range(1, NZ):
        start(rank_z(step))
    low_part[...] = times_transposed(act_rows[...], fac[...])
    for step in range(1, ROWS):
        start(low_s(step))

    near(0)
    own(2)
    near_partner(0)

    for step in range(1, NZ):
        rank_z(step).wait_recv()
    rank_all[y, core] = jnp.sum(rank_part[...].astype(F32), axis=0).astype(BF16)
    for step in range(1, NY):
        start(rank_y(step))
    total = low_part[pl.ds(pl.multiple_of(r * 8, 8), 8), :]
    for step in range(1, ROWS):
        low_s(step).wait_recv()
        total = total + low_piece[step]
    low_sum[r] = total
    for step in range(1, ROWS):
        start(low_g(step))

    near(1)
    own(3)
    near_partner(1)

    for step in range(1, ROWS):
        low_g(step).wait_recv()
    low_all[c] = low_sum[...].reshape(own_tok, 128).astype(BF16)
    for step in range(1, NZ):
        start(low_z(step))
    for step in range(1, NY):
        rank_y(step).wait_recv()
    start(rank_p())

    for load in loads[8:]:
        load.wait()
    far_in(0)
    product(0)
    z_step(0, 0)
    near(2)
    near_partner(2)

    rank_p().wait_recv()
    total = factor * lax.dot_general(
        act_cols[...],
        rank_all[...].reshape(group_tok, 128),
        (((0,), (0,)), ((), ())),
        preferred_element_type=F32,
    )
    ga_send[...] = total.reshape(NX, sub // NX, 128)
    for step in range(1, NX):
        start(ga_copy(step))
    adapter[...] = ADAPTER_SCALE * jnp.dot(
        rank_all[c // 2, c % 2], fac[...], preferred_element_type=F32
    )

    z_step(0, 1)
    far_in(1)
    product(1)
    z_step(1, 0)
    z_step(0, 2)
    near(3)
    near_partner(3)
    z_step(1, 1)
    z_step(0, 3)
    far_in(2)
    product(2)
    z_step(2, 0)
    z_step(1, 2)

    for step in range(1, NX):
        ga_copy(step).wait_recv()
    total = ga_send[x]
    for step in range(1, NX):
        total = total + ga_recv[step]
    ga_gate[...] = total[:, 0:64]
    ga_up[...] = total[:, 64:128]
    for step in range(1, NZ):
        low_z(step).wait_recv()

    z_last(0)
    z_step(2, 1)
    z_step(1, 3)
    far_in(3)
    product(3)
    z_step(3, 0)
    z_step(2, 2)

    mine = hid // ROWS
    piece = mine // NX
    window = 384
    base = jnp.minimum((r * mine) // 128 * 128, hid - window)
    shift = r * mine - base
    gate_sum = jnp.zeros((64, window), F32)
    up_sum = jnp.zeros((64, window), F32)
    for q in range(n_chunk):
        low_t = low_all[:, q * CHUNK : (q + 1) * CHUNK, :].reshape(ROWS * CHUNK, 128).T
        gate_sum += jnp.dot(
            low_t[0:64],
            d[q, :, :, pl.ds(pl.multiple_of(base, 128), window)].reshape(ROWS * CHUNK, window),
            preferred_element_type=F32,
        )
        up_sum += jnp.dot(
            low_t[64:128],
            d[q, :, :, pl.ds(pl.multiple_of(hid + base, 128), window)].reshape(
                ROWS * CHUNK, window
            ),
            preferred_element_type=F32,
        )
    gate_sum = factor * gate_sum
    up_sum = factor * up_sum
    lane = lax.broadcasted_iota(jnp.int32, (64, 128), 1)
    for e in range(NX):
        at = shift + e * piece
        gate_at = pltpu.roll(gate_sum, window - at, 1)[:, 0:128]
        up_at = pltpu.roll(up_sum, (window + 64 - at) % window, 1)[:, 0:128]
        gb_send[e] = jnp.where(lane < 64, gate_at, up_at)
    for step in range(1, NX):
        start(gb_copy(step))

    z_step(3, 1)
    z_last(1)
    z_step(2, 3)
    z_step(3, 2)
    for step in range(1, NX):
        gb_copy(step).wait_recv()
    total = gb_send[x]
    for step in range(1, NX):
        total = total + gb_recv[step]
    gb_gate[...] = total[:, 0:piece]
    gb_up[...] = pltpu.roll(total, 64, 1)[:, 0:piece]
    z_step(3, 3)
    z_last(2)
    z_last(3)
    for copy in sent:
        copy.wait_send()


def on_device(
    acts, cot_hidden, gate_pre, up_pre, w_gate, w_up, gate_down_factor, up_down_factor, b_gate, b_up
):
    group_tok, width = acts.shape
    own_tok, hid = cot_hidden.shape
    n_chunk = own_tok // CHUNK
    dma = pltpu.SemaphoreType.DMA
    vmem = pltpu.VMEM
    return pl.pallas_call(
        kernel,
        out_shape=(
            jax.ShapeDtypeStruct((group_tok // NZ, width), BF16),
            jax.ShapeDtypeStruct((width // 32, 64), F32),
            jax.ShapeDtypeStruct((width // 32, 64), F32),
            jax.ShapeDtypeStruct((64, hid // 32), F32),
            jax.ShapeDtypeStruct((64, hid // 32), F32),
        ),
        in_specs=[pl.BlockSpec(memory_space=pl.ANY)] * 10,
        out_specs=tuple([pl.BlockSpec(memory_space=pltpu.VMEM)] * 5),
        scratch_shapes=[
            vmem((3, own_tok, hid), BF16),
            vmem((width, 2 * hid), BF16),
            vmem((128, 2 * hid), BF16),
            vmem((128, width), BF16),
            vmem((own_tok, width), BF16),
            vmem((group_tok, width // NZ), BF16),
            vmem((n_chunk, ROWS, CHUNK, 2 * hid), BF16),
            vmem((n_chunk, ROWS, CHUNK, width), F32),
            vmem((n_chunk, CHUNK, width), BF16),
            vmem((n_chunk, 4, CHUNK, width), BF16),
            vmem((n_chunk, 4, CHUNK, width), BF16),
            vmem((own_tok, width), F32),
            vmem((NZ, own_tok, 128), BF16),
            vmem((NY, 2, own_tok, 128), BF16),
            vmem((own_tok, 128), F32),
            vmem((ROWS, 8, 128), F32),
            vmem((ROWS, 8, 128), F32),
            vmem((NZ, own_tok, 128), BF16),
            vmem((NX, width // 32, 128), F32),
            vmem((NX, width // 32, 128), F32),
            vmem((NX, 64, 128), F32),
            vmem((NX, 64, 128), F32),
            dma((11,)),
            dma((n_chunk, 4)),
            dma((n_chunk, 4)),
            dma((n_chunk, 4)),
            dma((n_chunk, 4)),
            dma((n_chunk, 4, 2)),
            dma((n_chunk, 4, 2)),
            dma((NZ - 1,)),
            dma((NZ - 1,)),
            dma((NY - 1,)),
            dma((NY - 1,)),
            dma,
            dma,
            dma((ROWS - 1,)),
            dma((ROWS - 1,)),
            dma((ROWS - 1,)),
            dma((ROWS - 1,)),
            dma((NZ - 1,)),
            dma((NZ - 1,)),
            dma((NX - 1,)),
            dma((NX - 1,)),
            dma((NX - 1,)),
            dma((NX - 1,)),
        ],
        compiler_params=pltpu.CompilerParams(
            collective_id=0, has_side_effects=True, vmem_limit_bytes=48 * 1024 * 1024
        ),
    )(
        acts,
        cot_hidden,
        gate_pre,
        up_pre,
        w_gate,
        w_up,
        gate_down_factor.T,
        up_down_factor.T,
        b_gate,
        b_up,
    )


def solution(mesh):
    in_specs = (
        P("dp", "row"),
        P(("dp", "row"), "col"),
        P(("dp", "row"), "col"),
        P(("dp", "row"), "col"),
        P("row", "col"),
        P("row", "col"),
        P(),
        P(),
        P(None, "col"),
        P(None, "col"),
    )
    out_specs = (
        P(("dp", "col"), "row"),
        P(("row", "col", "dp"), None),
        P(("row", "col", "dp"), None),
        P(None, ("col", "row", "dp")),
        P(None, ("col", "row", "dp")),
    )
    return jax.shard_map(
        on_device, mesh=mesh, in_specs=in_specs, out_specs=out_specs, check_vma=False
    )
```

time: 256 us -> 78.3 us (0.31)
  waiting for transfers between devices: 144 us -> 0 us
  Pallas kernels: 0 us -> 65.8 us
  blocking collectives: 63.6 us -> 0 us
  matrix products: 24.8 us -> 0 us
  between operations: 16 us -> 0.66 us
  local copies, waits for them, and re-layouts: 2.94 us -> 11.5 us
    unnamed x7 -> x0, waiting for transfers between devices: 84.4 us -> none
    pallas_call x0 -> x1, Pallas kernels: none -> 65.8 us  [on_device(): pl.pallas_call(kernel, out_shape=(jax.ShapeDtypeStruct((group_tok // NZ,...]
    psum x2 -> x0, blocking collectives: 63.6 us -> none  [the longest x1 33.6 us: on_device(): lax.psum((multiply_transposed(full_gate, b_gate), multiply_transposed(ful...]
    reduce_scatter x3 -> x0, waiting for transfers between devices: 40.2 us -> none  [the longest x1 25.7 us: on_device(): lax.psum_scatter(factor * trans_times(acts_sub, gate_rank_projection), 'd...]
    dot_general x12 -> x0, matrix products: 24.8 us -> none  [the longest x6 18.7 us: multiply_transposed(): lax.dot_general(left, right, (((1,), (1,)), ((), ())), preferred_element_...]
    all_gather x2 -> x0, waiting for transfers between devices: 19.9 us -> none  [the longest x1 19.8 us: on_device(): lax.all_gather(own_up, 'row', axis=0, tiled=True)]
    unnamed x18 -> x21, local copies, waits for them, and re-layouts: 2.94 us -> 11.5 us
  transfers between devices with their start and end apart: 6 -> 0, of which waited for: 4 -> 0; matrix products, arithmetic and copies ran while one was open for 11% -> 0% of each run, Pallas kernels for 0% -> 0%
where the time goes in v1:
time: 78.3 us; the launch traced here: 77.9 us
  Pallas kernels  65.8 us (84%)
  local copies, waits for them, and re-layouts  11.5 us (15%)
    pallas_call x1, Pallas kernels, on_device(): pl.pallas_call(kernel, out_shape=(jax.ShapeDtypeStruct((group_tok // NZ,...  65.8 us
    unnamed x21, local copies, waits for them, and re-layouts  11.5 us

profile of v1, /device:TPU:6, one launch (start us, length us, event | category | flops | bytes accessed | tf_op | source)
XLA Modules:
  0.0 77.9 jit_solution(12773035682326378342)
XLA Ops:
  0.6 0.0 copy-start
  0.6 1.2 %copy-done = bf16[512,1024]{1,0:T(8,128)(2,1)S(1)} copy-done((bf16[512,1024]{1,0:T(8,128)(2,1)S(1)}, bf16[512,1024]{1,0:T(8,128)(2,1)}, u32[]{:S(2)}) %copy-start) | copy-done | bytes 1048600
  1.9 0.0 copy-start.1
  1.9 1.2 %copy-done.1 = bf16[8192,64]{0,1:T(8,128)(2,1)S(1)} copy-done((bf16[8192,64]{0,1:T(8,128)(2,1)S(1)}, bf16[8192,64]{0,1:T(8,128)(2,1)}, u32[]{:S(2)}) %copy-start.1) | copy-done | bytes 1048600
  3.1 0.0 copy-start.2
  3.1 1.2 %copy-done.2 = bf16[8192,64]{0,1:T(8,128)(2,1)S(1)} copy-done((bf16[8192,64]{0,1:T(8,128)(2,1)S(1)}, bf16[8192,64]{0,1:T(8,128)(2,1)}, u32[]{:S(2)}) %copy-start.2) | copy-done | bytes 1048600
  4.3 0.0 copy-start.3
  4.3 0.9 %copy-done.3 = bf16[64,1920]{1,0:T(8,128)(2,1)S(1)} copy-done((bf16[64,1920]{1,0:T(8,128)(2,1)S(1)}, bf16[64,1920]{1,0:T(8,128)(2,1)}, u32[]{:S(2)}) %copy-start.3) | copy-done | bytes 245784
  5.3 0.0 copy-start.4
  5.3 0.9 %copy-done.4 = bf16[64,1920]{1,0:T(8,128)(2,1)S(1)} copy-done((bf16[64,1920]{1,0:T(8,128)(2,1)S(1)}, bf16[64,1920]{1,0:T(8,128)(2,1)}, u32[]{:S(2)}) %copy-start.4) | copy-done | bytes 245784
  6.2 0.0 copy-start.5
  6.2 0.9 %copy-done.5 = bf16[64,1920]{1,0:T(8,128)(2,1)S(1)} copy-done((bf16[64,1920]{1,0:T(8,128)(2,1)S(1)}, bf16[64,1920]{1,0:T(8,128)(2,1)}, u32[]{:S(2)}) %copy-start.5) | copy-done | bytes 245784
  7.1 0.0 copy-start.6
  7.1 0.9 %copy-done.6 = bf16[64,1920]{1,0:T(8,128)(2,1)S(1)} copy-done((bf16[64,1920]{1,0:T(8,128)(2,1)S(1)}, bf16[64,1920]{1,0:T(8,128)(2,1)}, u32[]{:S(2)}) %copy-start.6) | copy-done | bytes 245784
  8.1 0.0 copy-start.7
  8.1 0.9 %copy-done.7 = bf16[64,1920]{1,0:T(8,128)(2,1)S(1)} copy-done((bf16[64,1920]{1,0:T(8,128)(2,1)S(1)}, bf16[64,1920]{1,0:T(8,128)(2,1)}, u32[]{:S(2)}) %copy-start.7) | copy-done | bytes 245784
  9.0 65.8 %shard_map.137 = (bf16[64,1024]{1,0:T(8,128)(2,1)S(1)}, f32[32,64]{1,0:T(8,128)S(1)}, f32[32,64]{1,0:T(8,128)S(1)}, f32[64,60]{1,0:T(8,128)S(1)}, f32[64,60]{1,0:T(8,128)S(1)}) custom-call(bf16[512,1024]{1,0:T(8,128)(2,1)S(1)} %copy-done, bf16[64,1920]{1,0:T(8,128)(2,1)S(1)} %copy-done.3, bf16[64,1920]{1,0:T(8,128)(2,1)S(1)} %copy-done.4, ...), custom_call_target="tpu_custom_call" | custom-call | tf_op jit(solution)/shard_map/pallas_call | solution.py:452
  74.8 0.7 copy.20
  75.5 0.6 copy.21
  76.1 0.6 copy.22
  76.7 0.6 copy.23
  77.3 0.6 copy.24
Async XLA Ops:
  0.6 1.2 %copy-start = (bf16[512,1024]{1,0:T(8,128)(2,1)S(1)}, bf16[512,1024]{1,0:T(8,128)(2,1)}, u32[]{:S(2)}) copy-start(bf16[512,1024]{1,0:T(8,128)(2,1)} %acts.1) | copy-start | bytes 3145732
  1.9 1.2 %copy-start.1 = (bf16[8192,64]{0,1:T(8,128)(2,1)S(1)}, bf16[8192,64]{0,1:T(8,128)(2,1)}, u32[]{:S(2)}) copy-start(bf16[8192,64]{0,1:T(8,128)(2,1)} %param.16) | copy-start | bytes 3145732
  3.1 1.2 %copy-start.2 = (bf16[8192,64]{0,1:T(8,128)(2,1)S(1)}, bf16[8192,64]{0,1:T(8,128)(2,1)}, u32[]{:S(2)}) copy-start(bf16[8192,64]{0,1:T(8,128)(2,1)} %param.17) | copy-start | bytes 3145732
  4.3 0.9 %copy-start.3 = (bf16[64,1920]{1,0:T(8,128)(2,1)S(1)}, bf16[64,1920]{1,0:T(8,128)(2,1)}, u32[]{:S(2)}) copy-start(bf16[64,1920]{1,0:T(8,128)(2,1)} %cot.1) | copy-start | bytes 737284
  5.3 0.9 %copy-start.4 = (bf16[64,1920]{1,0:T(8,128)(2,1)S(1)}, bf16[64,1920]{1,0:T(8,128)(2,1)}, u32[]{:S(2)}) copy-start(bf16[64,1920]{1,0:T(8,128)(2,1)} %gate_pre.1) | copy-start | bytes 737284
  6.2 0.9 %copy-start.5 = (bf16[64,1920]{1,0:T(8,128)(2,1)S(1)}, bf16[64,1920]{1,0:T(8,128)(2,1)}, u32[]{:S(2)}) copy-start(bf16[64,1920]{1,0:T(8,128)(2,1)} %up_pre.1) | copy-start | bytes 737284
  7.1 0.9 %copy-start.6 = (bf16[64,1920]{1,0:T(8,128)(2,1)S(1)}, bf16[64,1920]{1,0:T(8,128)(2,1)}, u32[]{:S(2)}) copy-start(bf16[64,1920]{1,0:T(8,128)(2,1)} %b_gate.1) | copy-start | bytes 737284
  8.1 0.9 %copy-start.7 = (bf16[64,1920]{1,0:T(8,128)(2,1)S(1)}, bf16[64,1920]{1,0:T(8,128)(2,1)}, u32[]{:S(2)}) copy-start(bf16[64,1920]{1,0:T(8,128)(2,1)} %b_up.1) | copy-start | bytes 737284

commit v2 on v1

v2 whole, which is shorter than its diff:
```python
import jax
import jax.numpy as jnp
from jax import lax
from jax.experimental import pallas as pl
from jax.experimental.pallas import tpu as pltpu
from jax.sharding import PartitionSpec as P

MESH = pl.DeviceIdType.MESH
F32, BF16 = jnp.float32, jnp.bfloat16
ADAPTER_SCALE = 2.0
NY, NZ, NX = 4, 8, 4
ROWS = 2 * NY
CHUNK = 16


def times_transposed(left, right):
    return lax.dot_general(
        left, right, (((1,), (1,)), ((), ())), preferred_element_type=F32
    )


def kernel(
    acts,
    cot,
    gate_pre,
    up_pre,
    w_gate,
    w_up,
    gate_factor,
    up_factor,
    b_gate,
    b_up,
    out,
    ga_gate,
    ga_up,
    gb_gate,
    gb_up,
    pre,
    w,
    wt,
    b,
    fac,
    act_rows,
    act_cols,
    d,
    part,
    part_send,
    part_recv,
    half_recv,
    adapter,
    rank_part,
    rank_all,
    low_part,
    low_pair,
    low_chip,
    low_recv,
    low_all,
    ga_send,
    ga_recv,
    gb_send,
    gb_recv,
    in_sem,
    y_sem,
    po_sem,
    p_sem,
    z_sem,
    rz_sem,
    ry_sem,
    rp_sem,
    lp_sem,
    ly_sem,
    lz_sem,
    lq_sem,
    ga_sem,
    gb_sem,
):
    own_tok, hid = cot.shape
    group_tok, width = acts.shape
    n_chunk = own_tok // CHUNK
    factor = 2.0 / (group_tok * NX)
    r, c, x = lax.axis_index("row"), lax.axis_index("col"), lax.axis_index("dp")
    y, core = r // 2, r % 2
    sub = width // NZ
    half_tok = own_tok // 2
    near_half = pl.ds(pl.multiple_of(core * half_tok, half_tok), half_tok)
    far_half = pl.ds(pl.multiple_of((1 - core) * half_tok, half_tok), half_tok)

    width_at = pl.multiple_of(r * width, width)
    loads = [
        (cot, pre.at[0]),
        (gate_pre, pre.at[1]),
        (up_pre, pre.at[2]),
        (b_gate, b.at[0:64, 0:hid]),
        (b_up, b.at[64:128, hid : 2 * hid]),
        (acts.at[pl.ds(pl.multiple_of(c * own_tok, own_tok), own_tok), :], act_rows),
        (gate_factor.at[:, pl.ds(width_at, width)], fac.at[0:64]),
        (up_factor.at[:, pl.ds(width_at, width)], fac.at[64:128]),
        (w_gate, w.at[:, 0:hid]),
        (w_up, w.at[:, hid : 2 * hid]),
        (acts.at[:, pl.ds(pl.multiple_of(c * sub, sub), sub)], act_cols),
    ]
    loads = [pltpu.make_async_copy(src, dst, in_sem.at[i]) for i, (src, dst) in enumerate(loads)]
    for load in loads:
        load.start()

    y_peer = [None] + [{"row": ((y + step) % NY) * 2 + core} for step in range(1, NY)]
    z_peer = [None] + [{"col": (c + step) % NZ} for step in range(1, NZ)]
    x_peer = [None] + [{"dp": (x + step) % NX} for step in range(1, NX)]
    partner = {"row": y * 2 + (1 - core)}
    peers = [partner] + y_peer[1:] + z_peer[1:] + x_peer[1:]
    barrier = pltpu.get_barrier_semaphore()
    for peer in peers:
        pl.semaphore_signal(barrier, 1, device_id=peer, device_id_type=MESH)

    sent = []

    def remote(src, dst, sem, where):
        return pltpu.make_async_remote_copy(
            src_ref=src,
            dst_ref=dst,
            send_sem=sem.at[0],
            recv_sem=sem.at[1],
            device_id=where,
            device_id_type=MESH,
        )

    def start(copy):
        copy.start()
        sent.append(copy)

    def cotangents(q):
        rows = slice(q * CHUNK, (q + 1) * CHUNK)
        gate = pre[1, rows, :].astype(F32)
        sig = jax.nn.sigmoid(gate)
        hot = pre[0, rows, :].astype(F32)
        up = pre[2, rows, :].astype(F32)
        d[q, y, core, :, 0:hid] = (hot * up * sig * (1.0 + gate * (1.0 - sig))).astype(BF16)
        d[q, y, core, :, hid : 2 * hid] = (hot * gate * sig).astype(BF16)

    right, left, far = (y + 1) % NY, (y + NY - 1) % NY, (y + 2) % NY

    def y_copy(q, kind):
        ref, step = (
            (d.at[q, y, core], 1),
            (d.at[q, y, core], NY - 1),
            (d.at[q, left, core, :, 0:hid], 1),
            (d.at[q, right, core, :, hid : 2 * hid], NY - 1),
        )[kind]
        return remote(ref, ref, y_sem.at[q, kind], y_peer[step])

    def p_own():
        ref = d.at[:, y, core]
        return remote(ref, ref, po_sem, partner)

    def p_copy(q, kind):
        ref = d.at[q, (left, right, far)[kind], core]
        return remote(ref, ref, p_sem.at[q, kind], partner)

    def own(q):
        start(y_copy(q, 0))
        start(y_copy(q, 1))

    def near(q):
        y_copy(q, 0).wait_recv()
        start(y_copy(q, 2))
        y_copy(q, 1).wait_recv()
        start(y_copy(q, 3))
        if q + 2 < n_chunk:
            own(q + 2)
        start(p_copy(q, 0))
        start(p_copy(q, 1))

    def far_in(q):
        y_copy(q, 2).wait_recv()
        y_copy(q, 3).wait_recv()
        start(p_copy(q, 2))

    def product(q):
        if q == 0:
            p_own().wait_recv()
        for kind in range(NY - 1):
            p_copy(q, kind).wait_recv()
        tile = jnp.dot(
            d[q].reshape(ROWS * CHUNK, 2 * hid), wt[...], preferred_element_type=F32
        ).reshape(ROWS, CHUNK, width)
        part[q] = tile
        part_send[q] = tile.astype(BF16)
        for kind in range(6):
            start(z_copy(q, kind))

    lower, upper = slice(0, width // 2), slice(width // 2, width)

    def z_copy(q, kind):
        sem = z_sem.at[q, kind]
        at = [(c + step) % NZ for step in range(NZ)]
        if kind == 0:
            return remote(part_send.at[q, at[4], :, lower], half_recv.at[q, 0], sem, z_peer[6])
        if kind == 1:
            return remote(part_send.at[q, at[4], :, upper], half_recv.at[q, 1], sem, z_peer[2])
        if kind == 2:
            return remote(part_send.at[q, at[5]], part_recv.at[q, 0], sem, z_peer[7])
        if kind == 3:
            return remote(part_send.at[q, at[3]], part_recv.at[q, 1], sem, z_peer[1])
        if kind == 4:
            return remote(part_send.at[q, at[7]], part_recv.at[q, 2], sem, z_peer[7])
        if kind == 5:
            return remote(part_send.at[q, at[1]], part_recv.at[q, 3], sem, z_peer[1])
        if kind == 6:
            return remote(part_send.at[q, at[6]], part_recv.at[q, 4], sem, z_peer[6])
        return remote(part_send.at[q, at[2]], part_recv.at[q, 5], sem, z_peer[2])

    def z_on(q):
        for side, (same, other, step) in enumerate(((lower, upper, 6), (upper, lower, 2))):
            at = (c + step) % NZ
            z_copy(q, 2 + side).wait_recv()
            z_copy(q, side).wait_recv()
            total = part[q, at, :, same] + part_recv[q, side, :, same].astype(F32)
            total = total + half_recv[q, side].astype(F32)
            part_send[q, at, :, same] = total.astype(BF16)
            total = part[q, at, :, other] + part_recv[q, side, :, other].astype(F32)
            part_send[q, at, :, other] = total.astype(BF16)
            start(z_copy(q, 6 + side))

    def z_last(q):
        rows = slice(q * CHUNK, (q + 1) * CHUNK)
        total = part[q, c] + adapter[rows, :]
        for kind in range(4, 8):
            z_copy(q, kind).wait_recv()
            total = total + part_recv[q, kind - 2].astype(F32)
        out[rows, :] = total.astype(BF16)

    def rank_z(step):
        ref = rank_part.at[c]
        return remote(ref, ref, rz_sem.at[step - 1], z_peer[step])

    def rank_y(step):
        ref = rank_all.at[y, core]
        return remote(ref, ref, ry_sem.at[step - 1], y_peer[step])

    def rank_p():
        ref = rank_all.at[:, core]
        return remote(ref, ref, rp_sem, partner)

    def low_p():
        return remote(low_part.at[far_half], low_pair, lp_sem, partner)

    def low_y(step):
        return remote(low_chip, low_recv.at[step - 1], ly_sem.at[step - 1], y_peer[step])

    def low_z(step):
        ref = low_all.at[c, near_half]
        return remote(ref, ref, lz_sem.at[step - 1], z_peer[step])

    def low_q():
        ref = low_all.at[:, near_half]
        return remote(ref, ref, lq_sem, partner)

    def ga_copy(step):
        return remote(
            ga_send.at[(x + step) % NX], ga_recv.at[step - 1], ga_sem.at[step - 1], x_peer[step]
        )

    def gb_copy(step):
        return remote(
            gb_send.at[(x + step) % NX], gb_recv.at[step - 1], gb_sem.at[step - 1], x_peer[step]
        )

    for load in loads[0:3]:
        load.wait()
    for q in range(n_chunk):
        cotangents(q)
    b[0:64, hid : 2 * hid] = jnp.zeros((64, hid), BF16)
    b[64:128, 0:hid] = jnp.zeros((64, hid), BF16)
    for load in loads[3:8]:
        load.wait()
    rank_part[c] = times_transposed(d[:, y, core].reshape(own_tok, 2 * hid), b[...]).astype(BF16)
    low_part[...] = times_transposed(act_rows[...], fac[...])

    pl.semaphore_wait(barrier, len(peers))
    own(0)
    start(p_own())
    for step in range(1, NZ):
        start(rank_z(step))
    start(low_p())
    own(1)

    for load in loads[8:]:
        load.wait()

    @pl.loop(0, 2 * hid // 256)
    def _(n):
        at = pl.ds(pl.multiple_of(n * 256, 256), 256)
        wt[at, :] = w[:, at].T

    low_p().wait_recv()
    low_own = low_part[near_half, :] + low_pair[...]
    low_chip[...] = low_own.astype(BF16)
    for step in range(1, NY):
        start(low_y(step))
    total = rank_part[c].astype(F32)
    for step in range(1, NZ):
        rank_z(step).wait_recv()
        total = total + rank_part[(c + NZ - step) % NZ].astype(F32)
    rank_all[y, core] = total.astype(BF16)
    for step in range(1, NY):
        start(rank_y(step))

    near(0)
    for step in range(1, NY):
        low_y(step).wait_recv()
        low_own = low_own + low_recv[step - 1].astype(F32)
    low_all[c, near_half] = low_own.astype(BF16)
    for step in range(1, NZ):
        start(low_z(step))
    near(1)
    for step in range(1, NY):
        rank_y(step).wait_recv()
    start(rank_p())
    far_in(0)
    product(0)
    near(2)
    for step in range(1, NZ):
        low_z(step).wait_recv()
    start(low_q())
    far_in(1)
    product(1)

    rank_p().wait_recv()
    total = factor * lax.dot_general(
        act_cols[...],
        rank_all[...].reshape(group_tok, 128),
        (((0,), (0,)), ((), ())),
        preferred_element_type=F32,
    )
    ga_send[...] = total.reshape(NX, sub // NX, 128)
    for step in range(1, NX):
        start(ga_copy(step))
    adapter[...] = ADAPTER_SCALE * jnp.dot(
        rank_all[c // 2, c % 2], fac[...], preferred_element_type=F32
    )

    z_on(0)
    near(3)
    far_in(2)
    product(2)
    z_on(1)
    far_in(3)
    product(3)
    z_on(2)
    low_q().wait_recv()

    mine = hid // ROWS
    piece = mine // NX
    window = 384
    base = jnp.minimum((r * mine) // 128 * 128, hid - window)
    shift = r * mine - base
    gate_sum = jnp.zeros((64, window), F32)
    up_sum = jnp.zeros((64, window), F32)
    for q in range(n_chunk):
        low_t = low_all[:, q * CHUNK : (q + 1) * CHUNK, :].reshape(ROWS * CHUNK, 128).T
        at = pl.ds(pl.multiple_of(base, 128), window)
        gate_sum += jnp.dot(
            low_t[0:64],
            d[q, :, :, :, at].reshape(ROWS * CHUNK, window),
            preferred_element_type=F32,
        )
        at = pl.ds(pl.multiple_of(hid + base, 128), window)
        up_sum += jnp.dot(
            low_t[64:128],
            d[q, :, :, :, at].reshape(ROWS * CHUNK, window),
            preferred_element_type=F32,
        )
    gate_sum = factor * gate_sum
    up_sum = factor * up_sum
    lane = lax.broadcasted_iota(jnp.int32, (64, 128), 1)
    for e in range(NX):
        at = shift + e * piece
        gate_at = pltpu.roll(gate_sum, window - at, 1)[:, 0:128]
        up_at = pltpu.roll(up_sum, (window + 64 - at) % window, 1)[:, 0:128]
        gb_send[e] = jnp.where(lane < 64, gate_at, up_at)
    for step in range(1, NX):
        start(gb_copy(step))

    total = ga_send[x]
    for step in range(1, NX):
        ga_copy(step).wait_recv()
        total = total + ga_recv[step - 1]
    ga_gate[...] = total[:, 0:64]
    ga_up[...] = total[:, 64:128]
    z_last(0)
    z_last(1)
    z_on(3)
    z_last(2)
    total = gb_send[x]
    for step in range(1, NX):
        gb_copy(step).wait_recv()
        total = total + gb_recv[step - 1]
    gb_gate[...] = total[:, 0:piece]
    gb_up[...] = pltpu.roll(total, 64, 1)[:, 0:piece]
    z_last(3)
    for copy in sent:
        copy.wait_send()


def on_device(
    acts, cot_hidden, gate_pre, up_pre, w_gate, w_up, gate_down_factor, up_down_factor, b_gate, b_up
):
    group_tok, width = acts.shape
    own_tok, hid = cot_hidden.shape
    n_chunk = own_tok // CHUNK
    dma = pltpu.SemaphoreType.DMA
    vmem = pltpu.VMEM
    return pl.pallas_call(
        kernel,
        out_shape=(
            jax.ShapeDtypeStruct((group_tok // NZ, width), BF16),
            jax.ShapeDtypeStruct((width // 32, 64), F32),
            jax.ShapeDtypeStruct((width // 32, 64), F32),
            jax.ShapeDtypeStruct((64, hid // 32), F32),
            jax.ShapeDtypeStruct((64, hid // 32), F32),
        ),
        in_specs=[pl.BlockSpec(memory_space=pl.ANY)] * 10,
        out_specs=tuple([pl.BlockSpec(memory_space=pltpu.VMEM)] * 5),
        scratch_shapes=[
            vmem((3, own_tok, hid), BF16),
            vmem((width, 2 * hid), BF16),
            vmem((2 * hid, width), BF16),
            vmem((128, 2 * hid), BF16),
            vmem((128, width), BF16),
            vmem((own_tok, width), BF16),
            vmem((group_tok, width // NZ), BF16),
            vmem((n_chunk, NY, 2, CHUNK, 2 * hid), BF16),
            vmem((n_chunk, ROWS, CHUNK, width), F32),
            vmem((n_chunk, ROWS, CHUNK, width), BF16),
            vmem((n_chunk, 6, CHUNK, width), BF16),
            vmem((n_chunk, 2, CHUNK, width // 2), BF16),
            vmem((own_tok, width), F32),
            vmem((NZ, own_tok, 128), BF16),
            vmem((NY, 2, own_tok, 128), BF16),
            vmem((own_tok, 128), F32),
            vmem((own_tok // 2, 128), F32),
            vmem((own_tok // 2, 128), BF16),
            vmem((NY - 1, own_tok // 2, 128), BF16),
            vmem((NZ, own_tok, 128), BF16),
            vmem((NX, width // 32, 128), F32),
            vmem((NX - 1, width // 32, 128), F32),
            vmem((NX, 64, 128), F32),
            vmem((NX - 1, 64, 128), F32),
            dma((11,)),
            dma((n_chunk, 4, 2)),
            dma((2,)),
            dma((n_chunk, NY - 1, 2)),
            dma((n_chunk, 8, 2)),
            dma((NZ - 1, 2)),
            dma((NY - 1, 2)),
            dma((2,)),
            dma((2,)),
            dma((NY - 1, 2)),
            dma((NZ - 1, 2)),
            dma((2,)),
            dma((NX - 1, 2)),
            dma((NX - 1, 2)),
        ],
        compiler_params=pltpu.CompilerParams(
            collective_id=0, has_side_effects=True, vmem_limit_bytes=60 * 1024 * 1024
        ),
    )(
        acts,
        cot_hidden,
        gate_pre,
        up_pre,
        w_gate,
        w_up,
        gate_down_factor.T,
        up_down_factor.T,
        b_gate,
        b_up,
    )


def solution(mesh):
    in_specs = (
        P("dp", "row"),
        P(("dp", "row"), "col"),
        P(("dp", "row"), "col"),
        P(("dp", "row"), "col"),
        P("row", "col"),
        P("row", "col"),
        P(),
        P(),
        P(None, "col"),
        P(None, "col"),
    )
    out_specs = (
        P(("dp", "col"), "row"),
        P(("row", "col", "dp"), None),
        P(("row", "col", "dp"), None),
        P(None, ("col", "row", "dp")),
        P(None, ("col", "row", "dp")),
    )
    return jax.shard_map(
        on_device, mesh=mesh, in_specs=in_specs, out_specs=out_specs, check_vma=False
    )
```

time: 78.3 us -> 51.1 us (0.65)
  Pallas kernels: 65.8 us -> 43.1 us
  local copies, waits for them, and re-layouts: 11.5 us -> 6.96 us
    pallas_call x1, Pallas kernels: 65.8 us -> 43.1 us  [on_device(): pl.pallas_call(kernel, out_shape=(jax.ShapeDtypeStruct((group_tok // NZ,...]
    unnamed x21 -> x5, local copies, waits for them, and re-layouts: 11.5 us -> 6.96 us
where the time goes in v2:
time: 51.1 us; the launch traced here: 50.8 us
  Pallas kernels  43.1 us (84%)
  local copies, waits for them, and re-layouts  6.96 us (14%)
  between operations  0.65 us (1%)
    pallas_call x1, Pallas kernels, on_device(): pl.pallas_call(kernel, out_shape=(jax.ShapeDtypeStruct((group_tok // NZ,...  43.1 us
    unnamed x5, local copies, waits for them, and re-layouts  6.96 us

profile of v2, /device:TPU:6, one launch (start us, length us, event | category | flops | bytes accessed | tf_op | source)
XLA Modules:
  0.0 50.8 jit_solution(6416594146586279797)
XLA Ops:
  0.6 43.1 %shard_map.137 = (bf16[64,1024]{1,0:T(8,128)(2,1)}, f32[32,64]{1,0:T(8,128)}, f32[32,64]{1,0:T(8,128)}, f32[64,60]{1,0:T(8,128)}, f32[64,60]{1,0:T(8,128)}) custom-call(bf16[512,1024]{1,0:T(8,128)(2,1)} %acts.1, bf16[64,1920]{1,0:T(8,128)(2,1)} %cot.1, bf16[64,1920]{1,0:T(8,128)(2,1)} %gate_pre.1, bf16[64,1920]{1,0:T(8,128)(2,1)} %up_pre.1, ...), custom_call_target="tpu_custom_call" | custom-call | tf_op jit(solution)/shard_map/pallas_call | solution.py:413
  43.8 1.6 %copy.20 = bf16[64,1024]{1,0:T(8,128)(2,1)} copy(bf16[64,1024]{1,0:T(8,128)(2,1)} %get-tuple-element.10) | data formatting | bytes 262144
  45.4 1.3 %copy.21 = f32[32,64]{1,0:T(8,128)} copy(f32[32,64]{1,0:T(8,128)} %get-tuple-element.11) | data formatting | bytes 16384
  46.7 1.3 %copy.22 = f32[32,64]{1,0:T(8,128)} copy(f32[32,64]{1,0:T(8,128)} %get-tuple-element.12) | data formatting | bytes 16384
  48.0 1.4 %copy.23 = f32[64,60]{1,0:T(8,128)} copy(f32[64,60]{1,0:T(8,128)} %get-tuple-element.13) | data formatting | bytes 30720
  49.4 1.4 %copy.24 = f32[64,60]{1,0:T(8,128)} copy(f32[64,60]{1,0:T(8,128)} %get-tuple-element.14) | data formatting | bytes 30720

commit v3 on v2

--- a/solution.py
+++ b/solution.py
@@ -31,10 +31,7 @@
     b_gate,
     b_up,
     out,
-    ga_gate,
-    ga_up,
-    gb_gate,
-    gb_up,
+    small,
     pre,
     w,
     wt,
@@ -100,7 +97,7 @@
         (acts.at[:, pl.ds(pl.multiple_of(c * sub, sub), sub)], act_cols),
     ]
     loads = [pltpu.make_async_copy(src, dst, in_sem.at[i]) for i, (src, dst) in enumerate(loads)]
-    for load in loads:
+    for load in loads[0:8]:
         load.start()
 
     y_peer = [None] + [{"row": ((y + step) % NY) * 2 + core} for step in range(1, NY)]
@@ -140,11 +137,14 @@
     right, left, far = (y + 1) % NY, (y + NY - 1) % NY, (y + 2) % NY
 
     def y_copy(q, kind):
+        gate, up = slice(0, hid), slice(hid, 2 * hid)
         ref, step = (
-            (d.at[q, y, core], 1),
-            (d.at[q, y, core], NY - 1),
-            (d.at[q, left, core, :, 0:hid], 1),
-            (d.at[q, right, core, :, hid : 2 * hid], NY - 1),
+            (d.at[q, y, core, :, gate], 1),
+            (d.at[q, y, core, :, up], NY - 1),
+            (d.at[q, y, core, :, up], 1),
+            (d.at[q, y, core, :, gate], NY - 1),
+            (d.at[q, left, core, :, gate], 1),
+            (d.at[q, right, core, :, up], NY - 1),
         )[kind]
         return remote(ref, ref, y_sem.at[q, kind], y_peer[step])
 
@@ -157,22 +157,24 @@
         return remote(ref, ref, p_sem.at[q, kind], partner)
 
     def own(q):
-        start(y_copy(q, 0))
-        start(y_copy(q, 1))
+        for kind in range(4):
+            start(y_copy(q, kind))
 
     def near(q):
         y_copy(q, 0).wait_recv()
-        start(y_copy(q, 2))
+        start(y_copy(q, 4))
         y_copy(q, 1).wait_recv()
-        start(y_copy(q, 3))
+        start(y_copy(q, 5))
         if q + 2 < n_chunk:
             own(q + 2)
+        y_copy(q, 2).wait_recv()
+        y_copy(q, 3).wait_recv()
         start(p_copy(q, 0))
         start(p_copy(q, 1))
 
     def far_in(q):
-        y_copy(q, 2).wait_recv()
-        y_copy(q, 3).wait_recv()
+        y_copy(q, 4).wait_recv()
+        y_copy(q, 5).wait_recv()
         start(p_copy(q, 2))
 
     def product(q):
@@ -267,36 +269,50 @@
 
     for load in loads[0:3]:
         load.wait()
-    for q in range(n_chunk):
-        cotangents(q)
+    for load in loads[8:]:
+        load.start()
+    cotangents(0)
+    pl.semaphore_wait(barrier, len(peers))
+    own(0)
+    cotangents(1)
+    own(1)
+    cotangents(2)
+    cotangents(3)
+    start(p_own())
     b[0:64, hid : 2 * hid] = jnp.zeros((64, hid), BF16)
     b[64:128, 0:hid] = jnp.zeros((64, hid), BF16)
     for load in loads[3:8]:
         load.wait()
+    low_part[...] = times_transposed(act_rows[...], fac[...])
+    start(low_p())
     rank_part[c] = times_transposed(d[:, y, core].reshape(own_tok, 2 * hid), b[...]).astype(BF16)
-    low_part[...] = times_transposed(act_rows[...], fac[...])
-
-    pl.semaphore_wait(barrier, len(peers))
-    own(0)
-    start(p_own())
     for step in range(1, NZ):
         start(rank_z(step))
-    start(low_p())
-    own(1)
-
-    for load in loads[8:]:
-        load.wait()
-
-    @pl.loop(0, 2 * hid // 256)
-    def _(n):
-        at = pl.ds(pl.multiple_of(n * 256, 256), 256)
-        wt[at, :] = w[:, at].T
 
     low_p().wait_recv()
     low_own = low_part[near_half, :] + low_pair[...]
     low_chip[...] = low_own.astype(BF16)
     for step in range(1, NY):
         start(low_y(step))
+    near(0)
+
+    for load in loads[8:]:
+        load.wait()
+
+    @pl.loop(0, 2 * hid // 256)
+    def _(n):
+        at = pl.ds(pl.multiple_of(n * 256, 256), 256)
+        wt[at, :] = w[:, at].T
+
+    near(1)
+    for step in range(1, NY):
+        low_y(step).wait_recv()
+        low_own = low_own + low_recv[step - 1].astype(F32)
+    low_all[c, near_half] = low_own.astype(BF16)
+    for step in range(1, NZ):
+        start(low_z(step))
+    far_in(0)
+    product(0)
     total = rank_part[c].astype(F32)
     for step in range(1, NZ):
         rank_z(step).wait_recv()
@@ -304,49 +320,22 @@
     rank_all[y, core] = total.astype(BF16)
     for step in range(1, NY):
         start(rank_y(step))
-
-    near(0)
-    for step in range(1, NY):
-        low_y(step).wait_recv()
-        low_own = low_own + low_recv[step - 1].astype(F32)
-    low_all[c, near_half] = low_own.astype(BF16)
+    near(2)
+    far_in(1)
+    product(1)
+    near(3)
     for step in range(1, NZ):
-        start(low_z(step))
-    near(1)
+        low_z(step).wait_recv()
+    start(low_q())
+    far_in(2)
+    z_on(0)
+    far_in(3)
+    product(2)
+    product(3)
     for step in range(1, NY):
         rank_y(step).wait_recv()
     start(rank_p())
-    far_in(0)
-    product(0)
-    near(2)
-    for step in range(1, NZ):
-        low_z(step).wait_recv()
-    start(low_q())
-    far_in(1)
-    product(1)
-
-    rank_p().wait_recv()
-    total = factor * lax.dot_general(
-        act_cols[...],
-        rank_all[...].reshape(group_tok, 128),
-        (((0,), (0,)), ((), ())),
-        preferred_element_type=F32,
-    )
-    ga_send[...] = total.reshape(NX, sub // NX, 128)
-    for step in range(1, NX):
-        start(ga_copy(step))
-    adapter[...] = ADAPTER_SCALE * jnp.dot(
-        rank_all[c // 2, c % 2], fac[...], preferred_element_type=F32
-    )
-
-    z_on(0)
-    near(3)
-    far_in(2)
-    product(2)
     z_on(1)
-    far_in(3)
-    product(3)
-    z_on(2)
     low_q().wait_recv()
 
     mine = hid // ROWS
@@ -381,25 +370,47 @@
     for step in range(1, NX):
         start(gb_copy(step))
 
+    rank_p().wait_recv()
+    total = factor * lax.dot_general(
+        act_cols[...],
+        rank_all[...].reshape(group_tok, 128),
+        (((0,), (0,)), ((), ())),
+        preferred_element_type=F32,
+    )
+    ga_send[...] = total.reshape(NX, sub // NX, 128)
+    for step in range(1, NX):
+        start(ga_copy(step))
+    adapter[...] = ADAPTER_SCALE * jnp.dot(
+        rank_all[c // 2, c % 2], fac[...], preferred_element_type=F32
+    )
+
+    z_on(2)
+    z_last(0)
+    z_last(1)
+    z_on(3)
+    total = gb_send[x]
+    for step in range(1, NX):
+        gb_copy(step).wait_recv()
+        total = total + gb_recv[step - 1]
+    small[sub // NX :, :] = total
     total = ga_send[x]
     for step in range(1, NX):
         ga_copy(step).wait_recv()
         total = total + ga_recv[step - 1]
-    ga_gate[...] = total[:, 0:64]
-    ga_up[...] = total[:, 64:128]
-    z_last(0)
-    z_last(1)
-    z_on(3)
+    small[0 : sub // NX, :] = total
     z_last(2)
-    total = gb_send[x]
-    for step in range(1, NX):
-        gb_copy(step).wait_recv()
-        total = total + gb_recv[step - 1]
-    gb_gate[...] = total[:, 0:piece]
-    gb_up[...] = pltpu.roll(total, 64, 1)[:, 0:piece]
     z_last(3)
     for copy in sent:
         copy.wait_send()
+
+
+def place(out_in, small, out, ga_gate, ga_up, gb_gate, gb_up):
+    rows, piece = ga_gate.shape[0], gb_gate.shape[1]
+    out[...] = out_in[...]
+    ga_gate[...] = small[0:rows, 0:64]
+    ga_up[...] = small[0:rows, 64:128]
+    gb_gate[...] = small[rows:, 0:piece]
+    gb_up[...] = pltpu.roll(small[rows:, :], 64, 1)[:, 0:piece]
 
 
 def on_device(
@@ -410,17 +421,18 @@
     n_chunk = own_tok // CHUNK
     dma = pltpu.SemaphoreType.DMA
     vmem = pltpu.VMEM
-    return pl.pallas_call(
+    shapes = (
+        jax.ShapeDtypeStruct((group_tok // NZ, width), BF16),
+        jax.ShapeDtypeStruct((width // 32, 64), F32),
+        jax.ShapeDtypeStruct((width // 32, 64), F32),
+        jax.ShapeDtypeStruct((64, hid // 32), F32),
+        jax.ShapeDtypeStruct((64, hid // 32), F32),
+    )
+    results = pl.pallas_call(
         kernel,
-        out_shape=(
-            jax.ShapeDtypeStruct((group_tok // NZ, width), BF16),
-            jax.ShapeDtypeStruct((width // 32, 64), F32),
-            jax.ShapeDtypeStruct((width // 32, 64), F32),
-            jax.ShapeDtypeStruct((64, hid // 32), F32),
-            jax.ShapeDtypeStruct((64, hid // 32), F32),
-        ),
+        out_shape=(shapes[0], jax.ShapeDtypeStruct((width // 32 + 64, 128), F32)),
         in_specs=[pl.BlockSpec(memory_space=pl.ANY)] * 10,
-        out_specs=tuple([pl.BlockSpec(memory_space=pltpu.VMEM)] * 5),
+        out_specs=(pl.BlockSpec(memory_space=pltpu.VMEM),) * 2,
         scratch_shapes=[
             vmem((3, own_tok, hid), BF16),
             vmem((width, 2 * hid), BF16),
@@ -447,7 +459,7 @@
             vmem((NX, 64, 128), F32),
             vmem((NX - 1, 64, 128), F32),
             dma((11,)),
-            dma((n_chunk, 4, 2)),
+            dma((n_chunk, 6, 2)),
             dma((2,)),
             dma((n_chunk, NY - 1, 2)),
             dma((n_chunk, 8, 2)),
@@ -476,6 +488,12 @@
         b_gate,
         b_up,
     )
+    return pl.pallas_call(
+        place,
+        out_shape=shapes,
+        in_specs=[pl.BlockSpec(memory_space=pltpu.VMEM)] * 2,
+        out_specs=(pl.BlockSpec(memory_space=pltpu.VMEM),) * 5,
+    )(*results)
 
 
 def solution(mesh):

time: 51.1 us -> 47 us (0.920)
  local copies, waits for them, and re-layouts: 6.96 us -> 0 us
  Pallas kernels: 43.1 us -> 46.1 us
    unnamed x5 -> x0, local copies, waits for them, and re-layouts: 6.96 us -> none
    pallas_call x1 -> x2, Pallas kernels: 43.1 us -> 46.1 us  [the longest x1 44.5 us: on_device(): pl.pallas_call(kernel, out_shape=(shapes[0], jax.ShapeDtypeStruct((width...]
where the time goes in v3:
time: 47 us; the launch traced here: 46.8 us
  Pallas kernels  46.1 us (98%)
  between operations  0.64 us (1%)
    pallas_call x1, Pallas kernels, on_device(): pl.pallas_call(kernel, out_shape=(shapes[0], jax.ShapeDtypeStruct((width...  44.5 us
    pallas_call x1, Pallas kernels, on_device(): pl.pallas_call(place, out_shape=shapes, in_specs=[pl.BlockSpec(memory_spa...  1.6 us

profile of v3, /device:TPU:6, one launch (start us, length us, event | category | flops | bytes accessed | tf_op | source)
XLA Modules:
  0.0 46.8 jit_solution(578365698728773449)
XLA Ops:
  0.6 44.5 %shard_map.137 = (bf16[64,1024]{1,0:T(8,128)(2,1)}, f32[96,128]{1,0:T(8,128)}) custom-call(bf16[512,1024]{1,0:T(8,128)(2,1)} %acts.1, bf16[64,1920]{1,0:T(8,128)(2,1)} %cot.1, bf16[64,1920]{1,0:T(8,128)(2,1)} %gate_pre.1, bf16[64,1920]{1,0:T(8,128)(2,1)} %up_pre.1, bf16[1024,1920]{1,0:T(8,128)(2,1)} %w_gate.1, bf16[1024,1920]{1,0:T(8,128)(2,1)} %w_up.1, ...), custom_call_target="tpu_custom_call" | custom-call | tf_op jit(solution)/shard_map/pallas_call | solution.py:431
  45.2 1.6 %shard_map.138 = (bf16[64,1024]{1,0:T(8,128)(2,1)}, f32[32,64]{1,0:T(8,128)}, f32[32,64]{1,0:T(8,128)}, f32[64,60]{1,0:T(8,128)}, f32[64,60]{1,0:T(8,128)}) custom-call(bf16[64,1024]{1,0:T(8,128)(2,1)} %get-tuple-element.7.out_in, f32[96,128]{1,0:T(8,128)} %get-tuple-element.8.small), custom_call_target="tpu_custom_call" | custom-call | tf_op jit(solution)/shard_map/pallas_call | solution.py:491

commit v4 on v3

--- a/solution.py
+++ b/solution.py
@@ -323,19 +323,19 @@
     near(2)
     far_in(1)
     product(1)
+    z_on(0)
     near(3)
+    far_in(2)
+    product(2)
     for step in range(1, NZ):
         low_z(step).wait_recv()
     start(low_q())
-    far_in(2)
-    z_on(0)
-    far_in(3)
-    product(2)
-    product(3)
     for step in range(1, NY):
         rank_y(step).wait_recv()
     start(rank_p())
     z_on(1)
+    far_in(3)
+    product(3)
     low_q().wait_recv()
 
     mine = hid // ROWS

time: 47 us -> 45.1 us (0.960)
  Pallas kernels: 46.1 us -> 44.1 us
    pallas_call x1, Pallas kernels: 44.5 us -> 42.5 us  [on_device(): pl.pallas_call(kernel, out_shape=(shapes[0], jax.ShapeDtypeStruct((width...]
where the time goes in v4:
time: 45.1 us; the launch traced here: 44.8 us
  Pallas kernels  44.1 us (98%)
  between operations  0.64 us (1%)
    pallas_call x1, Pallas kernels, on_device(): pl.pallas_call(kernel, out_shape=(shapes[0], jax.ShapeDtypeStruct((width...  42.5 us
    pallas_call x1, Pallas kernels, on_device(): pl.pallas_call(place, out_shape=shapes, in_specs=[pl.BlockSpec(memory_spa...  1.6 us

profile of v4, /device:TPU:6, one launch (start us, length us, event | category | flops | bytes accessed | tf_op | source)
XLA Modules:
  0.0 44.8 jit_solution(15078132009479049359)
XLA Ops:
  0.6 42.5 %shard_map.137 = (bf16[64,1024]{1,0:T(8,128)(2,1)}, f32[96,128]{1,0:T(8,128)}) custom-call(bf16[512,1024]{1,0:T(8,128)(2,1)} %acts.1, bf16[64,1920]{1,0:T(8,128)(2,1)} %cot.1, bf16[64,1920]{1,0:T(8,128)(2,1)} %gate_pre.1, bf16[64,1920]{1,0:T(8,128)(2,1)} %up_pre.1, bf16[1024,1920]{1,0:T(8,128)(2,1)} %w_gate.1, bf16[1024,1920]{1,0:T(8,128)(2,1)} %w_up.1, ...), custom_call_target="tpu_custom_call" | custom-call | tf_op jit(solution)/shard_map/pallas_call | solution.py:431
  43.2 1.6 %shard_map.138 = (bf16[64,1024]{1,0:T(8,128)(2,1)}, f32[32,64]{1,0:T(8,128)}, f32[32,64]{1,0:T(8,128)}, f32[64,60]{1,0:T(8,128)}, f32[64,60]{1,0:T(8,128)}) custom-call(bf16[64,1024]{1,0:T(8,128)(2,1)} %get-tuple-element.7.out_in, f32[96,128]{1,0:T(8,128)} %get-tuple-element.8.small), custom_call_target="tpu_custom_call" | custom-call | tf_op jit(solution)/shard_map/pallas_call | solution.py:491

commit v5 on v4

--- a/solution.py
+++ b/solution.py
@@ -327,14 +327,14 @@
     near(3)
     far_in(2)
     product(2)
+    z_on(1)
+    far_in(3)
+    for step in range(1, NY):
+        rank_y(step).wait_recv()
+    start(rank_p())
     for step in range(1, NZ):
         low_z(step).wait_recv()
     start(low_q())
-    for step in range(1, NY):
-        rank_y(step).wait_recv()
-    start(rank_p())
-    z_on(1)
-    far_in(3)
     product(3)
     low_q().wait_recv()
 

time: 45.1 us -> 45.2 us (level)
  no operation moved by 1% of the time
where the time goes in v5:
time: 45.2 us; the launch traced here: 45.1 us
  Pallas kernels  44.4 us (98%)
  between operations  0.64 us (1%)
    pallas_call x1, Pallas kernels, on_device(): pl.pallas_call(kernel, out_shape=(shapes[0], jax.ShapeDtypeStruct((width...  42.8 us
    pallas_call x1, Pallas kernels, on_device(): pl.pallas_call(place, out_shape=shapes, in_specs=[pl.BlockSpec(memory_spa...  1.6 us

profile of v5, /device:TPU:6, one launch (start us, length us, event | category | flops | bytes accessed | tf_op | source)
XLA Modules:
  0.0 45.1 jit_solution(10682449038010834805)
XLA Ops:
  0.6 42.8 %shard_map.137 = (bf16[64,1024]{1,0:T(8,128)(2,1)}, f32[96,128]{1,0:T(8,128)}) custom-call(bf16[512,1024]{1,0:T(8,128)(2,1)} %acts.1, bf16[64,1920]{1,0:T(8,128)(2,1)} %cot.1, bf16[64,1920]{1,0:T(8,128)(2,1)} %gate_pre.1, bf16[64,1920]{1,0:T(8,128)(2,1)} %up_pre.1, bf16[1024,1920]{1,0:T(8,128)(2,1)} %w_gate.1, bf16[1024,1920]{1,0:T(8,128)(2,1)} %w_up.1, ...), custom_call_target="tpu_custom_call" | custom-call | tf_op jit(solution)/shard_map/pallas_call | solution.py:431
  43.5 1.6 %shard_map.138 = (bf16[64,1024]{1,0:T(8,128)(2,1)}, f32[32,64]{1,0:T(8,128)}, f32[32,64]{1,0:T(8,128)}, f32[64,60]{1,0:T(8,128)}, f32[64,60]{1,0:T(8,128)}) custom-call(bf16[64,1024]{1,0:T(8,128)(2,1)} %get-tuple-element.7.out_in, f32[96,128]{1,0:T(8,128)} %get-tuple-element.8.small), custom_call_target="tpu_custom_call" | custom-call | tf_op jit(solution)/shard_map/pallas_call | solution.py:491
